TPU v7x, 32 devices: a whole 2x2x4 slice. The times are simulated.
32 devices in a mesh: groups: 2 (over x), blk: 4 (over y, core), ref: 4 (over z).
Axes of the slice: x: 2, y: 2, z: 4, core: 2. Of those that a mesh axis runs over, the one named last changes fastest.
Arguments:
- queries: bfloat16 [4096, 1024], P(('groups', 'blk')), parts along dimension 0, may hold values from -4 to 4
- references: bfloat16 [8192, 1024], P(('groups', 'blk', 'ref')), parts along dimension 0, may hold values from -4 to 4
- labels: bfloat16 [8192, 512], P(('groups', 'blk', 'ref')), parts along dimension 0, may hold values from 0.0009994507 to 1
Outputs:
- log_scores: float32 [4096, 512], P(('groups', 'blk', 'ref')), parts along dimension 0
There are 2 independent parts, one for each index of `groups`. A program takes and returns all parts, laid end to end along the dimension named above; each array names one. Nothing has to cross between parts.
All inputs are finite; a program needn't handle non-finite values.
Results may differ from a plain program's by a relative error of at most 0.007.
Values may be sent and summed in bfloat16 or wider, within the bound.
A program may use at most 128 MiB of HBM per device.

v0:
```python
import math

import jax
import jax.numpy as jnp
from jax import lax
from jax.sharding import PartitionSpec as P

NEG_FLOOR = -1e30


def merged(value, axis, join):
    pieces = jax.tree.map(lambda part: lax.all_gather(part, axis), value)
    head = jax.tree.map(lambda part: part[0], pieces)
    tail = jax.tree.map(lambda part: part[1:], pieces)
    subtotal, _ = lax.scan(lambda subtotal, piece: (join(subtotal, piece), None), head, tail)
    return subtotal


def absorb(running, queries, ref_rows, label_rows, score_scale):
    row_top, row_total, row_mass = running
    scores = (
        lax.dot_general(
            queries, ref_rows, (((1,), (1,)), ((), ())), preferred_element_type=jnp.float32
        )
        * score_scale
    )
    new_top = jnp.maximum(row_top, jnp.max(scores, axis=1))
    shrink = jnp.exp(row_top - new_top)
    weights = jnp.exp(scores - new_top[:, None]).astype(jnp.bfloat16)
    row_total = row_total * shrink + jnp.sum(weights.astype(jnp.float32), axis=1)
    row_mass = row_mass * shrink[:, None] + jnp.dot(
        weights, label_rows, preferred_element_type=jnp.float32
    )
    return (new_top, row_total, row_mass)


def combine(first, second):
    new_top = jnp.maximum(first[0], second[0])
    scale_first = jnp.exp(first[0] - new_top)
    scale_second = jnp.exp(second[0] - new_top)
    row_total = first[1] * scale_first + second[1] * scale_second
    row_mass = first[2] * scale_first[:, None] + second[2] * scale_second[:, None]
    return (new_top, row_total, row_mass)


def per_device(queries, references, labels):
    width = queries.shape[1]
    classes = labels.shape[1]
    query_rows = queries.shape[0]
    score_scale = 2.0 / math.sqrt(width)
    initial = (
        jnp.full((query_rows,), NEG_FLOOR, jnp.float32),
        jnp.zeros((query_rows,), jnp.float32),
        jnp.zeros((query_rows, classes), jnp.float32),
    )
    running = initial
    ref_part = lax.all_gather(references, "blk", axis=0, tiled=True)
    label_part = lax.all_gather(labels, "blk", axis=0, tiled=True)
    count = ref_part.shape[0]
    span = math.gcd(count, 512)
    grouped_refs = ref_part.reshape(count // span, span, width)
    grouped_labels = label_part.reshape(count // span, span, classes)

    def advance(current, members):
        return (absorb(current, queries, members[0], members[1], score_scale), None)

    running, unused = lax.scan(advance, running, (grouped_refs, grouped_labels))
    row_top, row_total, row_mass = running
    share = query_rows // lax.axis_size("ref")
    row_top, row_total, row_mass = merged((row_top, row_total, row_mass), "ref", combine)
    offset = lax.axis_index("ref") * share
    mass_rows = lax.dynamic_slice_in_dim(row_mass, offset, share, 0)
    total_rows = lax.dynamic_slice_in_dim(row_total, offset, share, 0)
    return jnp.log(mass_rows) - jnp.log(total_rows)[:, None]


def solution(mesh):
    return jax.shard_map(
        per_device,
        mesh=mesh,
        in_specs=(
            P(("groups", "blk"), None),
            P(("groups", "blk", "ref"), None),
            P(("groups", "blk", "ref"), None),
        ),
        out_specs=P(("groups", "blk", "ref"), None),
        check_vma=False,
    )
```

profile of v0, /device:TPU:0, one launch (start us, length us, event | category | flops | bytes accessed | tf_op | source)
XLA Modules:
  0.0 158.3 jit_solution(7280220137814239432)
XLA Ops:
  6.5 0.0 all-gather.11.cloned.1.call-start
  6.5 0.7 all-gather.11.cloned.1.call-update
  7.3 0.0 all-gather.9.cloned.1.call-start
  7.3 0.7 all-gather.9.cloned.1.call-update
  8.0 0.0 all-gather.13.cloned.1.call-start
  8.1 20.3 %all-gather.11.cloned.1.call-done = bf16[1024,512]{1,0:T(8,128)(2,1)} async-done(((bf16[256,512]{1,0:T(8,128)(2,1)}), bf16[1024,512]{1,0:T(8,128)(2,1)}) %all-gather.11.cloned.1.call-update) | async-done | bytes 1048592 | tf_op jit(solution)/shard_map/all_gather | solution.py:58
  28.4 24.2 %all-gather.9.cloned.1.call-done = bf16[1024,1024]{1,0:T(8,128)(2,1)} async-done(((bf16[256,1024]{1,0:T(8,128)(2,1)}), bf16[1024,1024]{1,0:T(8,128)(2,1)}) %all-gather.9.cloned.1.call-update) | async-done | bytes 2097168 | tf_op jit(solution)/shard_map/all_gather | solution.py:57
  52.6 6.3 %while.30 = (s32[]{:T(128)}, f32[512]{0:T(512)S(1)}, f32[512]{0:T(512)S(1)}, f32[512,512]{1,0:T(8,128)S(1)}, bf16[2,512,1024]{2,1,0:T(8,128)(2,1)}, /*index=5*/b...) while((s32[]{:T(128)}, f32[512]{0:T(512)S(1)}, f32[512]{0:T(512)S(1)}, ...), condition=%wide.region_3.4_spmd.clone, body=%wide.region_0.3_spmd.clone.sunk | while | flops 808192512 | bytes 12092041 | solution.py:67
  52.6 0.0 copy-start.1
  52.6 2.4 %fusion.18 = (f32[512]{0:T(512)S(1)}, f32[512,512]{1,0:T(8,128)S(1)}) fusion(bf16[512,1024]{1,0:T(8,128)(2,1)} %get-tuple-element.278, bf16[2,512,1024]{2,1,0:T(8,128)(2,1)} %get-tuple-element.277, s32[]{:T(128)} %get-tuple-element.264), kind=kOutput, calls=%fused_computation.26.clone.1 | convolution fusion | flops 537394688 | bytes 3148288 | tf_op jit(solution)/shard_map/while/body/eval_jaxpr/dot_general | solution.py:22
  55.0 0.2 convert_reduce_fusion.2
  55.2 0.0 copy-done.1
  55.2 0.5 convolution_add_fusion.2
  55.7 0.0 copy-start.1
  55.7 2.4 %fusion.18 = (f32[512]{0:T(512)S(1)}, f32[512,512]{1,0:T(8,128)S(1)}) fusion(bf16[512,1024]{1,0:T(8,128)(2,1)} %get-tuple-element.278, bf16[2,512,1024]{2,1,0:T(8,128)(2,1)} %get-tuple-element.277, s32[]{:T(128)} %get-tuple-element.264), kind=kOutput, calls=%fused_computation.26.clone.1 | convolution fusion | flops 537394688 | bytes 3148288 | tf_op jit(solution)/shard_map/while/body/eval_jaxpr/dot_general | solution.py:22
  58.1 0.2 convert_reduce_fusion.2
  58.4 0.0 copy-done.1
  58.4 0.5 convolution_add_fusion.2
  58.9 0.0 copy-start
  58.9 1.0 copy-done
  59.9 0.0 all-gather.13.cloned.1.call-update
  59.9 11.9 %all-gather.3 = f32[4,1,512]{2,1,0:T(1,128)S(1)} all-gather(f32[1,1,512]{2,1,0:T(1,128)S(1)} %bitcast.42), channel_id=2, replica_groups=mesh['groups'=2,'blk'=4,'ref'=4] {'ref'}, dimensions={0}, use_global_device_ids=true | all-gather | bytes 10240 | tf_op jit(solution)/shard_map/all_gather | solution.py:12
  71.8 12.0 %all-gather.4 = f32[4,1,512]{2,1,0:T(1,128)S(1)} all-gather(f32[1,1,512]{2,1,0:T(1,128)S(1)} %bitcast.45), channel_id=3, replica_groups=mesh['groups'=2,'blk'=4,'ref'=4] {'ref'}, dimensions={0}, use_global_device_ids=true | all-gather | bytes 10240 | tf_op jit(solution)/shard_map/all_gather | solution.py:12
  83.9 57.1 %all-gather.13.cloned.1.call-done = f32[2048,512]{1,0:T(8,128)} async-done(((f32[512,512]{1,0:T(8,128)}), f32[2048,512]{1,0:T(8,128)}) %all-gather.13.cloned.1.call-update) | async-done | bytes 4194320 | tf_op jit(solution)/shard_map/all_gather | solution.py:12
  140.9 3.9 %slice.39 = f32[1536,512]{1,0:T(8,128)} slice(f32[2048,512]{1,0:T(8,128)} %all-gather.13.cloned.1.call-done), slice={[512:2048], [0:512]} | slice | bytes 6291456 | tf_op jit(solution)/shard_map/slice | solution.py:14
  144.8 1.3 slice.36
  146.1 4.7 %while.29 = (s32[]{:T(128)}, f32[512]{0:T(512)S(1)}, f32[512]{0:T(512)S(1)}, f32[512,512]{1,0:T(8,128)S(1)}, f32[3,512]{1,0:T(4,128)S(1)}, /*index=5*/f32[3,512]{1,0:T(4,128)S(1)}, f32[3,512,512]{2,1,0:T(8,128)}, s32[]{:T(128)}) while((s32[]{:T(128)}, f32[512]{0:T(512)S(1)}, f32[512]{0:T(512)S(1)}, f32[512,512]{1,0:T(8,128)S(1)}, ...), condition=%wide.region_5.6_spmd, body=%wide.region_4.5_spmd.sunk | while | flops 789506 | bytes 3174493 | solution.py:15
  146.2 1.5 fusion.15
  147.7 1.5 fusion.15
  149.3 1.5 fusion.15
  150.8 0.1 dynamic-slice_log_fusion
  150.9 0.8 log_subtract_fusion
  (21 shorter events, 0.2 us)
Async XLA Ops:
  6.5 21.8 %all-gather.11.cloned.1.call-start = ((), (), s32[]{:S(2)}) async-start(), calls=%async_computation.1 | async-start | bytes 1310720 | tf_op jit(solution)/shard_map/all_gather | solution.py:58
  7.3 45.3 %all-gather.9.cloned.1.call-start = ((), (), s32[]{:S(2)}) async-start(), calls=%async_computation | async-start | bytes 2621440 | tf_op jit(solution)/shard_map/all_gather | solution.py:57
  8.0 132.9 %all-gather.13.cloned.1.call-start = ((), (), s32[]{:S(2)}) async-start(), calls=%async_computation.2 | async-start | bytes 5242880 | tf_op jit(solution)/shard_map/all_gather | solution.py:12
  52.6 2.6 %copy-start.1 = (bf16[2,512,512]{2,1,0:T(8,128)(2,1)S(1)}, bf16[2,512,512]{2,1,0:T(8,128)(2,1)}, u32[]{:S(2)}) copy-start(bf16[2,512,512]{2,1,0:T(8,128)(2,1)} %get-tuple-element.279) | copy-start | bytes 3145732 | tf_op jit(solution)/shard_map/while
  55.7 2.6 %copy-start.1 = (bf16[2,512,512]{2,1,0:T(8,128)(2,1)S(1)}, bf16[2,512,512]{2,1,0:T(8,128)(2,1)}, u32[]{:S(2)}) copy-start(bf16[2,512,512]{2,1,0:T(8,128)(2,1)} %get-tuple-element.279) | copy-start | bytes 3145732 | tf_op jit(solution)/shard_map/while
  58.9 1.0 copy-start
Sparse Core Ops, SparseCore 0:
  8.9 19.4 all-gather.10
  29.9 22.5 all-gather.8
  60.0 80.8 all-gather.12
where the time goes:
time: 159 us; the launch traced here: 158 us
  waiting for transfers between devices  103 us (65%)
  blocking collectives  24 us (15%)
  between operations  13.2 us (8%)
  local copies, waits for them, and re-layouts  6.26 us (4%)
  other arithmetic  5.86 us (4%)
  matrix products  5.78 us (4%)
    all_gather x1, waiting for transfers between devices, merged(): pieces = jax.tree.map(lambda part: lax.all_gather(part, axis), value)  57.1 us
    all_gather x1, waiting for transfers between devices, per_device(): ref_part = lax.all_gather(references, 'blk', axis=0, tiled=True)  24.2 us
    all_gather x2, blocking collectives, merged(): pieces = jax.tree.map(lambda part: lax.all_gather(part, axis), value)  24 us
    all_gather x1, waiting for transfers between devices, per_device(): label_part = lax.all_gather(labels, 'blk', axis=0, tiled=True)  20.3 us
    dot_general x2, matrix products, absorb(): lax.dot_general(queries, ref_rows, (((1,), (1,)), ((), ())), preferred_el...  4.77 us
    add x3, other arithmetic, combine(): first[2] * scale_first[:, None] + second[2] * scale_second[:, None]  4.56 us
    slice x3, local copies, waits for them, and re-layouts, merged(): tail = jax.tree.map(lambda part: part[1:], pieces)  3.87 us
  transfers between devices with their start and end apart: 3, of which 3 were waited for; matrix products, arithmetic and copies ran while one was open for 0% of the time, Pallas kernels for 0%

commit v1 on v0

v1 whole, which is shorter than its diff:
```python
import functools
import math

import jax
import jax.numpy as jnp
from jax import lax
from jax.experimental import pallas as pl
from jax.experimental.pallas import tpu as pltpu
from jax.sharding import PartitionSpec as P

MESH = pl.DeviceIdType.MESH
LANES = 128
VMEM_LIMIT = 52 * 1024 * 1024


def kernel(
    ny, cores, nz, score_scale,
    q_hbm, r_hbm, l_hbm, out_ref,
    q, refs, labs, scores, peak, wts, mass, stage, landed, stat_out, stat_in, wide,
    q_sem, own_sem, send_sem, recv_sem, zsend_sem, zrecv_sem, tsend_sem, trecv_sem,
):
    blk = lax.axis_index("blk")
    zi = lax.axis_index("ref")
    nb = ny * cores
    rows, width = r_hbm.shape
    classes = l_hbm.shape[1]
    nq = q_hbm.shape[0]
    share = nq // nz
    nr = rows // LANES
    nc = classes // LANES
    items = nr + nc
    yi, core = blk // cores, blk % cores
    sibling = yi * cores + (1 - core)

    def peer(d):
        return ((yi + d) % ny) * cores + core

    def zpeer(d):
        return (zi + d) % nz

    def ref_piece(slot, j):
        return refs.at[slot, pl.ds(pl.multiple_of(j * LANES, LANES), LANES)]

    def lab_piece(slot, c):
        return labs.at[c, pl.ds(pl.multiple_of(slot * rows, rows), rows)]

    def own_ref(j):
        return r_hbm.at[pl.ds(j * LANES, LANES)]

    def own_lab(c):
        return l_hbm.at[:, pl.ds(c * LANES, LANES)]

    def remote(src, dst, sent, slot, item, dev):
        return pltpu.make_async_remote_copy(
            src_ref=src, dst_ref=dst, send_sem=send_sem.at[sent, item], recv_sem=recv_sem.at[slot, item],
            device_id={"blk": dev}, device_id_type=MESH,
        )

    def to_peer_ref(d, j):
        slot = cores * (ny - d)
        return remote(own_ref(j), ref_piece(slot, j), cores * d, slot, j, peer(d))

    def to_peer_lab(d, c):
        slot = cores * (ny - d)
        return remote(own_lab(c), lab_piece(slot, c), cores * d, slot, nr + c, peer(d))

    def to_sib_ref(j):
        return remote(own_ref(j), ref_piece(1, j), 1, 1, j, sibling)

    def to_sib_lab(c):
        return remote(own_lab(c), lab_piece(1, c), 1, 1, nr + c, sibling)

    def pass_ref(d, j):
        return remote(ref_piece(cores * d, j), ref_piece(cores * d + 1, j), cores * d + 1, cores * d + 1, j, sibling)

    def pass_lab(d, c):
        return remote(lab_piece(cores * d, c), lab_piece(cores * d + 1, c), cores * d + 1, cores * d + 1, nr + c, sibling)

    def arrived_ref(slot, j):
        remote(ref_piece(slot, j), ref_piece(slot, j), slot, slot, j, sibling).wait_recv()

    def arrived_lab(slot, c):
        remote(lab_piece(slot, c), lab_piece(slot, c), slot, slot, nr + c, sibling).wait_recv()

    q_copy = pltpu.make_async_copy(q_hbm, q, q_sem)
    q_copy.start()
    own_copies = [pltpu.make_async_copy(own_ref(j), ref_piece(0, j), own_sem.at[j]) for j in range(nr)]
    own_copies += [pltpu.make_async_copy(own_lab(c), lab_piece(0, c), own_sem.at[nr + c]) for c in range(nc)]
    for copy in own_copies:
        copy.start()

    barrier = pltpu.get_barrier_semaphore()
    if cores == 2:
        pl.semaphore_signal(barrier, inc=1, device_id={"blk": sibling}, device_id_type=MESH)
    for d in range(1, ny):
        pl.semaphore_signal(barrier, inc=1, device_id={"blk": peer(d)}, device_id_type=MESH)
    for d in range(1, nz):
        pl.semaphore_signal(barrier, inc=1, device_id={"ref": zpeer(d)}, device_id_type=MESH)
    pl.semaphore_wait(barrier, cores - 1 + ny - 1 + nz - 1)

    for j in range(nr):
        for d in range(1, ny):
            to_peer_ref(d, j).start()
    if cores == 2:
        for j in range(nr):
            to_sib_ref(j).start()
    for c in range(nc):
        for d in range(1, ny):
            to_peer_lab(d, c).start()
    if cores == 2:
        for c in range(nc):
            to_sib_lab(c).start()

    peak[...] = jnp.full(peak.shape, -jnp.inf, jnp.float32)

    def score(slot, j):
        part = lax.dot_general(
            q[...], ref_piece(slot, j)[...], (((1,), (1,)), ((), ())), preferred_element_type=jnp.float32
        ) * score_scale
        scores[slot * nr + j] = part
        peak[...] = jnp.maximum(peak[...], part)

    q_copy.wait()
    for j in range(nr):
        own_copies[j].wait()

    def own_step(j, carry):
        score(0, j)
        return carry

    lax.fori_loop(0, nr, own_step, 0)

    if cores == 2:

        def sib_step(j, carry):
            arrived_ref(1, j)
            score(1, j)
            return carry

        lax.fori_loop(0, nr, sib_step, 0)

    def far_step(i, carry):
        d, j = 1 + i // nr, i % nr
        arrived_ref(cores * d, j)
        if cores == 2:
            pass_ref(d, j).start()
        score(cores * d, j)
        if cores == 2:
            arrived_ref(cores * d + 1, j)
            score(cores * d + 1, j)
        return carry

    lax.fori_loop(0, (ny - 1) * nr, far_step, 0)

    lane = lax.broadcasted_iota(jnp.int32, (LANES, LANES), 1)

    def weigh(t, carry):
        r = pl.ds(pl.multiple_of(t * LANES, LANES), LANES)
        top = jnp.broadcast_to(jnp.max(peak[r, :], axis=1, keepdims=True), (LANES, LANES))

        def one(i, total):
            w = jnp.exp(scores[i, r, :] - top).astype(jnp.bfloat16)
            wts[r, pl.ds(pl.multiple_of(i * LANES, LANES), LANES)] = w
            return total + w.astype(jnp.float32)

        total = lax.fori_loop(0, nb * nr, one, jnp.zeros((LANES, LANES), jnp.float32), unroll=nb * nr <= 8)
        total = jnp.broadcast_to(jnp.sum(total, axis=1, keepdims=True), (LANES, LANES))
        stat_out[:, r] = jnp.where(lane < 4, top, total).T[0:8]
        return carry

    lax.fori_loop(0, nq // LANES, weigh, 0)

    narrow = share % LANES == 0

    def stat_copy(d):
        to = zpeer(d)
        src = stat_out.at[:, pl.ds(pl.multiple_of(to * share, LANES), share)] if narrow else stat_out
        return pltpu.make_async_remote_copy(
            src_ref=src, dst_ref=stat_in.at[nz - d], send_sem=tsend_sem.at[d], recv_sem=trecv_sem.at[nz - d],
            device_id={"ref": to}, device_id_type=MESH,
        )

    def mass_copy(d, c):
        to = zpeer(d)
        return pltpu.make_async_remote_copy(
            src_ref=stage.at[c, pl.ds(pl.multiple_of(to * share, share), share)], dst_ref=landed.at[c, nz - d],
            send_sem=zsend_sem.at[d, c], recv_sem=zrecv_sem.at[nz - d, c],
            device_id={"ref": to}, device_id_type=MESH,
        )

    for d in range(1, nz):
        stat_copy(d).start()

    def mass_step(c, carry):
        def far_labels(d, carry):
            arrived_lab(cores * d, c)
            if cores == 2:
                pass_lab(d, c).start()
            return carry

        lax.fori_loop(1, ny, far_labels, 0)
        pltpu.make_async_copy(lab_piece(0, c), lab_piece(0, c), own_sem.at[nr + c]).wait()
        if cores == 2:

            def other_labels(d, carry):
                arrived_lab(cores * d + 1, c)
                return carry

            lax.fori_loop(0, ny, other_labels, 0)
        part = jnp.dot(wts[...], labs[c], preferred_element_type=jnp.float32)
        mass[c] = part
        stage[c] = part.astype(jnp.bfloat16)
        for d in range(1, nz):
            mass_copy(d, c).start()
        return carry

    lax.fori_loop(0, nc, mass_step, 0)

    mine = pl.ds(pl.multiple_of(zi * share, share), share)

    def spread(d, row):
        line = stat_in[d, row:row + 1, :] if d else None
        if d == 0:
            line = stat_out[row:row + 1, mine] if narrow else stat_out[row:row + 1, :]
        full = jnp.broadcast_to(line, (LANES, line.shape[1])).T
        if narrow:
            return full
        wide[...] = full
        return wide[mine, :]

    for d in range(1, nz):
        stat_copy(nz - d).wait_recv()
    tops = [spread(d, 0) for d in range(nz)]
    top = functools.reduce(jnp.maximum, tops)
    shrinks = [jnp.exp(t - top) for t in tops]
    total = sum(f * spread(d, 4) for d, f in enumerate(shrinks))
    log_total = jnp.log(total)

    for c in range(nc):
        acc = mass[c, mine, :] * shrinks[0]
        for d in range(1, nz):
            mass_copy(nz - d, c).wait_recv()
            acc += landed[c, d].astype(jnp.float32) * shrinks[d]
        out_ref[:, c * LANES:(c + 1) * LANES] = jnp.log(acc) - log_total

    for d in range(1, nz):
        stat_copy(d).wait_send()
        for c in range(nc):
            mass_copy(d, c).wait_send()
    for d in range(1, ny):
        for j in range(nr):
            to_peer_ref(d, j).wait_send()
            if cores == 2:
                pass_ref(d, j).wait_send()
        for c in range(nc):
            to_peer_lab(d, c).wait_send()
            if cores == 2:
                pass_lab(d, c).wait_send()
    if cores == 2:
        for j in range(nr):
            to_sib_ref(j).wait_send()
        for c in range(nc):
            to_sib_lab(c).wait_send()


def per_device(queries, references, labels):
    nq, width = queries.shape
    rows = references.shape[0]
    classes = labels.shape[1]
    nb, nz = lax.axis_size("blk"), lax.axis_size("ref")
    cores = 2 if nb % 2 == 0 else 1
    ny = nb // cores
    share = nq // nz
    nr, nc = rows // LANES, classes // LANES
    items = nr + nc
    score_scale = 2.0 / math.sqrt(width)
    stat_w = share if share % LANES == 0 else nq
    return pl.pallas_call(
        functools.partial(kernel, ny, cores, nz, score_scale),
        out_shape=jax.ShapeDtypeStruct((share, classes), jnp.float32),
        in_specs=[pl.BlockSpec(memory_space=pltpu.HBM)] * 3,
        out_specs=pl.BlockSpec(memory_space=pltpu.VMEM),
        scratch_shapes=[
            pltpu.VMEM((nq, width), jnp.bfloat16),
            pltpu.VMEM((nb, rows, width), jnp.bfloat16),
            pltpu.VMEM((nc, nb * rows, LANES), jnp.bfloat16),
            pltpu.VMEM((nb * nr, nq, LANES), jnp.float32),
            pltpu.VMEM((nq, LANES), jnp.float32),
            pltpu.VMEM((nq, nb * rows), jnp.bfloat16),
            pltpu.VMEM((nc, nq, LANES), jnp.float32),
            pltpu.VMEM((nc, nq, LANES), jnp.bfloat16),
            pltpu.VMEM((nc, nz, share, LANES), jnp.bfloat16),
            pltpu.VMEM((8, nq), jnp.float32),
            pltpu.VMEM((nz, 8, stat_w), jnp.float32),
            pltpu.VMEM((nq, LANES), jnp.float32),
            pltpu.SemaphoreType.DMA,
            pltpu.SemaphoreType.DMA((items,)),
            pltpu.SemaphoreType.DMA((nb, items)),
            pltpu.SemaphoreType.DMA((nb, items)),
            pltpu.SemaphoreType.DMA((nz, nc)),
            pltpu.SemaphoreType.DMA((nz, nc)),
            pltpu.SemaphoreType.DMA((nz,)),
            pltpu.SemaphoreType.DMA((nz,)),
        ],
        compiler_params=pltpu.CompilerParams(
            collective_id=0, has_side_effects=True, vmem_limit_bytes=VMEM_LIMIT
        ),
    )(queries, references, labels)


def solution(mesh):
    return jax.shard_map(
        per_device,
        mesh=mesh,
        in_specs=(
            P(("groups", "blk"), None),
            P(("groups", "blk", "ref"), None),
            P(("groups", "blk", "ref"), None),
        ),
        out_specs=P(("groups", "blk", "ref"), None),
        check_vma=False,
    )
```

time: 159 us -> 39.7 us (0.25)
  waiting for transfers between devices: 103 us -> 0 us
  Pallas kernels: 0 us -> 36.9 us
  blocking collectives: 24 us -> 0 us
  between operations: 13.2 us -> 0.01 us
  other arithmetic: 5.86 us -> 0 us
  matrix products: 5.78 us -> 0 us
  local copies, waits for them, and re-layouts: 6.26 us -> 2.7 us
    all_gather x3 -> x0, waiting for transfers between devices: 102 us -> none  [the longest x1 57.1 us: merged(): pieces = jax.tree.map(lambda part: lax.all_gather(part, axis), value)]
    pallas_call x0 -> x1, Pallas kernels: none -> 36.9 us  [per_device(): pl.pallas_call(functools.partial(kernel, ny, cores, nz, score_scale), out...]
    all_gather x2 -> x0, blocking collectives: 24 us -> none  [merged(): pieces = jax.tree.map(lambda part: lax.all_gather(part, axis), value)]
    dot_general x4 -> x0, matrix products: 5.78 us -> none  [the longest x2 4.77 us: absorb(): lax.dot_general(queries, ref_rows, (((1,), (1,)), ((), ())), preferred_el...]
    slice x6 -> x0, local copies, waits for them, and re-layouts: 5.16 us -> none  [the longest x3 3.87 us: merged(): tail = jax.tree.map(lambda part: part[1:], pieces)]
    add x8 -> x0, other arithmetic: 4.65 us -> none  [the longest x3 4.56 us: combine(): first[2] * scale_first[:, None] + second[2] * scale_second[:, None]]
    unnamed x4 -> x5, local copies, waits for them, and re-layouts: 0.97 us -> 2.7 us
  transfers between devices with their start and end apart: 3 -> 0, of which waited for: 3 -> 0; matrix products, arithmetic and copies ran while one was open for 0% -> 0% of each run, Pallas kernels for 0% -> 0%
where the time goes in v1:
time: 39.7 us; the launch traced here: 39.6 us
  Pallas kernels  36.9 us (93%)
  local copies, waits for them, and re-layouts  2.7 us (7%)
    pallas_call x1, Pallas kernels, per_device(): pl.pallas_call(functools.partial(kernel, ny, cores, nz, score_scale), out...  36.9 us
    unnamed x5, local copies, waits for them, and re-layouts  2.7 us

profile of v1, /device:TPU:0, one launch (start us, length us, event | category | flops | bytes accessed | tf_op | source)
XLA Modules:
  0.0 39.6 jit_solution(11354323821283568488)
XLA Ops:
  0.0 0.0 copy-start
  0.0 1.0 %copy-done = bf16[256,1024]{1,0:T(8,128)(2,1)S(1)} copy-done((bf16[256,1024]{1,0:T(8,128)(2,1)S(1)}, bf16[256,1024]{1,0:T(8,128)(2,1)}, u32[]{:S(2)}) %copy-start) | copy-done | bytes 524312
  1.0 0.0 copy-start.1
  1.0 0.9 %copy-done.1 = bf16[256,512]{1,0:T(8,128)(2,1)S(1)} copy-done((bf16[256,512]{1,0:T(8,128)(2,1)S(1)}, bf16[256,512]{1,0:T(8,128)(2,1)}, u32[]{:S(2)}) %copy-start.1) | copy-done | bytes 262168
  2.0 36.9 %shard_map.37 = f32[128,512]{1,0:T(8,128)S(1)} custom-call(bf16[512,1024]{1,0:T(8,128)(2,1)} %q_hbm.1, bf16[256,1024]{1,0:T(8,128)(2,1)S(1)} %copy-done, bf16[256,512]{1,0:T(8,128)(2,1)S(1)} %copy-done.1), custom_call_target="tpu_custom_call" | custom-call | tf_op jit(solution)/shard_map/pallas_call | solution.py:278
  38.9 0.7 %copy.5 = f32[128,512]{1,0:T(8,128)} copy(f32[128,512]{1,0:T(8,128)S(1)} %shard_map.37) | data formatting | bytes 524288
Async XLA Ops:
  0.0 1.0 %copy-start = (bf16[256,1024]{1,0:T(8,128)(2,1)S(1)}, bf16[256,1024]{1,0:T(8,128)(2,1)}, u32[]{:S(2)}) copy-start(bf16[256,1024]{1,0:T(8,128)(2,1)} %r_hbm.1) | copy-start | bytes 1572868
  1.0 0.9 %copy-start.1 = (bf16[256,512]{1,0:T(8,128)(2,1)S(1)}, bf16[256,512]{1,0:T(8,128)(2,1)}, u32[]{:S(2)}) copy-start(bf16[256,512]{1,0:T(8,128)(2,1)} %l_hbm.1) | copy-start | bytes 786436

commit v2 on v1

--- a/solution.py
+++ b/solution.py
@@ -10,13 +10,13 @@
 
 MESH = pl.DeviceIdType.MESH
 LANES = 128
-VMEM_LIMIT = 52 * 1024 * 1024
+VMEM_LIMIT = 64 * 1024 * 1024 - 256 * 1024
 
 
 def kernel(
     ny, cores, nz, score_scale,
     q_hbm, r_hbm, l_hbm, out_ref,
-    q, refs, labs, scores, peak, wts, mass, stage, landed, stat_out, stat_in, wide,
+    q, refs, labs, scores, peak, wts, mass, stage, stage_mid, landed, stat_out, stat_mid, stat_in, wide,
     q_sem, own_sem, send_sem, recv_sem, zsend_sem, zrecv_sem, tsend_sem, trecv_sem,
 ):
     blk = lax.axis_index("blk")
@@ -172,26 +172,90 @@
 
     narrow = share % LANES == 0
 
-    def stat_copy(d):
-        to = zpeer(d)
-        src = stat_out.at[:, pl.ds(pl.multiple_of(to * share, LANES), share)] if narrow else stat_out
+    merge = nz == 4 and narrow
+    half = zi // 2
+    mate = zi + 1 - 2 * (zi % 2)
+    inner = 2 - half
+    outer = 3 - 3 * half
+    is_end = (zi + half + 1) % 2
+
+    def rows_of(to):
+        return pl.ds(pl.multiple_of(to * share, share), share)
+
+    def stat_copy(src, kind, slot, to):
         return pltpu.make_async_remote_copy(
-            src_ref=src, dst_ref=stat_in.at[nz - d], send_sem=tsend_sem.at[d], recv_sem=trecv_sem.at[nz - d],
+            src_ref=src, dst_ref=stat_in.at[slot], send_sem=tsend_sem.at[kind], recv_sem=trecv_sem.at[slot],
             device_id={"ref": to}, device_id_type=MESH,
         )
 
-    def mass_copy(d, c):
-        to = zpeer(d)
+    def stat_rows(to):
+        return stat_out.at[:, rows_of(to)] if narrow else stat_out
+
+    def mass_copy(src, kind, slot, to, c):
         return pltpu.make_async_remote_copy(
-            src_ref=stage.at[c, pl.ds(pl.multiple_of(to * share, share), share)], dst_ref=landed.at[c, nz - d],
-            send_sem=zsend_sem.at[d, c], recv_sem=zrecv_sem.at[nz - d, c],
+            src_ref=src, dst_ref=landed.at[c, slot], send_sem=zsend_sem.at[kind, c], recv_sem=zrecv_sem.at[slot, c],
             device_id={"ref": to}, device_id_type=MESH,
         )
 
-    for d in range(1, nz):
-        stat_copy(d).start()
-
-    def mass_step(c, carry):
+    if merge:
+        plain = [(1, 1 + is_end, inner), (0, 0, mate)]
+    else:
+        plain = [(d, nz - d, zpeer(d)) for d in range(1, nz)]
+
+    def stat_plain(kind, slot, to):
+        return stat_copy(stat_rows(to), kind, slot, to)
+
+    def mass_plain(kind, slot, to, c):
+        return mass_copy(stage.at[c, rows_of(to)], kind, slot, to, c)
+
+    def stat_via():
+        return stat_copy(stat_rows(outer), 2, 3, mate)
+
+    def mass_via(c):
+        return mass_copy(stage.at[c, rows_of(outer)], 2, 3, mate, c)
+
+    def stat_both():
+        return stat_copy(stat_mid, 2, 1, outer)
+
+    def mass_both(c):
+        return mass_copy(stage_mid.at[c], 2, 1, outer, c)
+
+    def stat_arrived(slot):
+        stat_copy(stat_in.at[slot], 0, slot, mate if merge else zpeer(1)).wait_recv()
+
+    def mass_arrived(slot, c):
+        mass_copy(landed.at[c, slot], 0, slot, mate if merge else zpeer(1), c).wait_recv()
+
+    def across(line):
+        return jnp.broadcast_to(line, (LANES, line.shape[1])).T
+
+    def join_stats():
+        stat_arrived(3)
+        here = stat_out[:, rows_of(outer)]
+        there = stat_in[3]
+        top = jnp.maximum(here[0:4], there[0:4])
+        shrink_here = jnp.exp(here[0:4] - top)
+        shrink_there = jnp.exp(there[0:4] - top)
+        stat_mid[0:4, :] = top
+        stat_mid[4:8, :] = here[4:8] * shrink_here + there[4:8] * shrink_there
+        stat_both().start()
+        wide[0:share, :] = across(shrink_here[0:1])
+        wide[share:2 * share, :] = across(shrink_there[0:1])
+
+    def join_mass(c):
+        mass_arrived(3, c)
+        both = mass[c, rows_of(outer), :] * wide[0:share, :]
+        both += landed[c, 3].astype(jnp.float32) * wide[share:2 * share, :]
+        stage_mid[c] = both.astype(jnp.bfloat16)
+        mass_both(c).start()
+
+    if merge:
+        pl.when(is_end == 1)(lambda: stat_via().start())
+    for to in plain:
+        stat_plain(*to).start()
+
+    for c in range(nc):
+
         def far_labels(d, carry):
             arrived_lab(cores * d, c)
             if cores == 2:
@@ -199,7 +263,7 @@
             return carry
 
         lax.fori_loop(1, ny, far_labels, 0)
-        pltpu.make_async_copy(lab_piece(0, c), lab_piece(0, c), own_sem.at[nr + c]).wait()
+        own_copies[nr + c].wait()
         if cores == 2:
 
             def other_labels(d, carry):
@@ -210,43 +274,72 @@
         part = jnp.dot(wts[...], labs[c], preferred_element_type=jnp.float32)
         mass[c] = part
         stage[c] = part.astype(jnp.bfloat16)
-        for d in range(1, nz):
-            mass_copy(d, c).start()
-        return carry
-
-    lax.fori_loop(0, nc, mass_step, 0)
-
-    mine = pl.ds(pl.multiple_of(zi * share, share), share)
-
-    def spread(d, row):
-        line = stat_in[d, row:row + 1, :] if d else None
-        if d == 0:
+        if merge:
+            pl.when(is_end == 1)(lambda: mass_via(c).start())
+        for to in plain:
+            mass_plain(*to, c).start()
+        if merge:
+
+            @pl.when(is_end == 0)
+            def _():
+                if c == 0:
+                    join_stats()
+                else:
+                    join_mass(c - 1)
+                if c == nc - 1:
+                    join_mass(c)
+
+    mine = rows_of(zi)
+
+    def spread(slot, row):
+        if slot is None:
             line = stat_out[row:row + 1, mine] if narrow else stat_out[row:row + 1, :]
-        full = jnp.broadcast_to(line, (LANES, line.shape[1])).T
+        else:
+            line = stat_in[slot, row:row + 1, :]
+        full = across(line)
         if narrow:
             return full
         wide[...] = full
         return wide[mine, :]
 
-    for d in range(1, nz):
-        stat_copy(nz - d).wait_recv()
-    tops = [spread(d, 0) for d in range(nz)]
-    top = functools.reduce(jnp.maximum, tops)
-    shrinks = [jnp.exp(t - top) for t in tops]
-    total = sum(f * spread(d, 4) for d, f in enumerate(shrinks))
-    log_total = jnp.log(total)
-
-    for c in range(nc):
-        acc = mass[c, mine, :] * shrinks[0]
-        for d in range(1, nz):
-            mass_copy(nz - d, c).wait_recv()
-            acc += landed[c, d].astype(jnp.float32) * shrinks[d]
-        out_ref[:, c * LANES:(c + 1) * LANES] = jnp.log(acc) - log_total
-
-    for d in range(1, nz):
-        stat_copy(d).wait_send()
+    def finish(slots):
+        for slot in slots:
+            stat_arrived(slot)
+        senders = [None] + slots
+        tops = [spread(slot, 0) for slot in senders]
+        top = functools.reduce(jnp.maximum, tops)
+        shrinks = [jnp.exp(t - top) for t in tops]
+        total = sum(f * spread(slot, 4) for slot, f in zip(senders, shrinks))
+        log_total = jnp.log(total)
         for c in range(nc):
-            mass_copy(d, c).wait_send()
+            acc = mass[c, mine, :] * shrinks[0]
+            for slot, f in zip(slots, shrinks[1:]):
+                mass_arrived(slot, c)
+                acc += landed[c, slot].astype(jnp.float32) * f
+            out_ref[:, c * LANES:(c + 1) * LANES] = jnp.log(acc) - log_total
+
+    if merge:
+
+        @pl.when(is_end == 1)
+        def _():
+            finish([0, 1])
+            stat_via().wait_send()
+            for c in range(nc):
+                mass_via(c).wait_send()
+
+        @pl.when(is_end == 0)
+        def _():
+            finish([0, 1, 2])
+            stat_both().wait_send()
+            for c in range(nc):
+                mass_both(c).wait_send()
+    else:
+        finish(list(range(1, nz)))
+
+    for to in plain:
+        stat_plain(*to).wait_send()
+        for c in range(nc):
+            mass_plain(*to, c).wait_send()
     for d in range(1, ny):
         for j in range(nr):
             to_peer_ref(d, j).wait_send()
@@ -289,8 +382,10 @@
             pltpu.VMEM((nq, nb * rows), jnp.bfloat16),
             pltpu.VMEM((nc, nq, LANES), jnp.float32),
             pltpu.VMEM((nc, nq, LANES), jnp.bfloat16),
+            pltpu.VMEM((nc, share, LANES), jnp.bfloat16),
             pltpu.VMEM((nc, nz, share, LANES), jnp.bfloat16),
             pltpu.VMEM((8, nq), jnp.float32),
+            pltpu.VMEM((8, stat_w), jnp.float32),
             pltpu.VMEM((nz, 8, stat_w), jnp.float32),
             pltpu.VMEM((nq, LANES), jnp.float32),
             pltpu.SemaphoreType.DMA,

time: 39.7 us -> 38.6 us (0.972)
  local copies, waits for them, and re-layouts: 2.7 us -> 1.67 us
    unnamed x5 -> x1, local copies, waits for them, and re-layouts: 2.7 us -> 1.67 us
where the time goes in v2:
time: 38.6 us; the launch traced here: 38.5 us
  Pallas kernels  36.8 us (95%)
  local copies, waits for them, and re-layouts  1.67 us (4%)
    pallas_call x1, Pallas kernels, per_device(): pl.pallas_call(functools.partial(kernel, ny, cores, nz, score_scale), out...  36.8 us
    unnamed x1, local copies, waits for them, and re-layouts  1.67 us

profile of v2, /device:TPU:0, one launch (start us, length us, event | category | flops | bytes accessed | tf_op | source)
XLA Modules:
  0.0 38.5 jit_solution(10008805372644710204)
XLA Ops:
  0.0 36.8 %shard_map.37 = f32[128,512]{1,0:T(8,128)} custom-call(bf16[512,1024]{1,0:T(8,128)(2,1)} %q_hbm.1, bf16[256,1024]{1,0:T(8,128)(2,1)} %r_hbm.1, bf16[256,512]{1,0:T(8,128)(2,1)} %l_hbm.1), custom_call_target="tpu_custom_call" | custom-call | tf_op jit(solution)/shard_map/pallas_call | solution.py:371
  36.8 1.7 %copy.5 = f32[128,512]{1,0:T(8,128)} copy(f32[128,512]{1,0:T(8,128)} %shard_map.37) | data formatting | bytes 524288

commit v3 on v2

--- a/solution.py
+++ b/solution.py
@@ -16,7 +16,7 @@
 def kernel(
     ny, cores, nz, score_scale,
     q_hbm, r_hbm, l_hbm, out_ref,
-    q, refs, labs, scores, peak, wts, mass, stage, stage_mid, landed, stat_out, stat_mid, stat_in, wide,
+    q, refs, labs, scores, peak, first, wts, mass, stage, stage_mid, landed, stat_out, stat_mid, stat_in, wide,
     q_sem, own_sem, send_sem, recv_sem, zsend_sem, zrecv_sem, tsend_sem, trecv_sem,
 ):
     blk = lax.axis_index("blk")
@@ -139,6 +139,43 @@
 
         lax.fori_loop(0, nr, sib_step, 0)
 
+    lane = lax.broadcasted_iota(jnp.int32, (LANES, LANES), 1)
+    near = cores * nr
+
+    def tile(t):
+        return pl.ds(pl.multiple_of(t * LANES, LANES), LANES)
+
+    def weights_of(r, low, high):
+        top = jnp.broadcast_to(jnp.max(peak[r, :], axis=1, keepdims=True), (LANES, LANES))
+
+        def one(i, total):
+            w = jnp.exp(scores[i, r, :] - top).astype(jnp.bfloat16)
+            wts[r, pl.ds(pl.multiple_of(i * LANES, LANES), LANES)] = w
+            return total + w.astype(jnp.float32)
+
+        total = lax.fori_loop(low, high, one, jnp.zeros((LANES, LANES), jnp.float32), unroll=high - low <= 8)
+        return top, jnp.broadcast_to(jnp.sum(total, axis=1, keepdims=True), (LANES, LANES))
+
+    def weigh_near(t, carry):
+        r = tile(t)
+        top, total = weights_of(r, 0, near)
+        first[0, r, :] = top
+        first[1, r, :] = total
+        if ny == 1:
+            stat_out[:, r] = jnp.where(lane < 4, top, total).T[0:8]
+        return carry
+
+    def weigh_far(t, carry):
+        r = tile(t)
+        top, total = weights_of(r, near, nb * nr)
+        shrink = jnp.exp(first[0, r, :] - top)
+        first[0, r, :] = shrink
+        total += first[1, r, :] * shrink
+        stat_out[:, r] = jnp.where(lane < 4, top, total).T[0:8]
+        return carry
+
+    lax.fori_loop(0, nq // LANES, weigh_near, 0)
+
     def far_step(i, carry):
         d, j = 1 + i // nr, i % nr
         arrived_ref(cores * d, j)
@@ -152,23 +189,18 @@
 
     lax.fori_loop(0, (ny - 1) * nr, far_step, 0)
 
-    lane = lax.broadcasted_iota(jnp.int32, (LANES, LANES), 1)
-
-    def weigh(t, carry):
-        r = pl.ds(pl.multiple_of(t * LANES, LANES), LANES)
-        top = jnp.broadcast_to(jnp.max(peak[r, :], axis=1, keepdims=True), (LANES, LANES))
-
-        def one(i, total):
-            w = jnp.exp(scores[i, r, :] - top).astype(jnp.bfloat16)
-            wts[r, pl.ds(pl.multiple_of(i * LANES, LANES), LANES)] = w
-            return total + w.astype(jnp.float32)
-
-        total = lax.fori_loop(0, nb * nr, one, jnp.zeros((LANES, LANES), jnp.float32), unroll=nb * nr <= 8)
-        total = jnp.broadcast_to(jnp.sum(total, axis=1, keepdims=True), (LANES, LANES))
-        stat_out[:, r] = jnp.where(lane < 4, top, total).T[0:8]
-        return carry
-
-    lax.fori_loop(0, nq // LANES, weigh, 0)
+    def far_labels(c):
+        def one(d, carry):
+            arrived_lab(cores * d, c)
+            if cores == 2:
+                pass_lab(d, c).start()
+            return carry
+
+        lax.fori_loop(1, ny, one, 0)
+
+    far_labels(0)
+    if ny > 1:
+        lax.fori_loop(0, nq // LANES, weigh_far, 0)
 
     narrow = share % LANES == 0
 
@@ -256,13 +288,8 @@
 
     for c in range(nc):
 
-        def far_labels(d, carry):
-            arrived_lab(cores * d, c)
-            if cores == 2:
-                pass_lab(d, c).start()
-            return carry
-
-        lax.fori_loop(1, ny, far_labels, 0)
+        if c > 0:
+            far_labels(c)
         own_copies[nr + c].wait()
         if cores == 2:
 
@@ -271,7 +298,12 @@
                 return carry
 
             lax.fori_loop(0, ny, other_labels, 0)
-        part = jnp.dot(wts[...], labs[c], preferred_element_type=jnp.float32)
+        split = cores * rows
+        part = jnp.dot(wts[:, 0:split], labs[c, 0:split, :], preferred_element_type=jnp.float32)
+        if ny > 1:
+            part = part * first[0] + jnp.dot(
+                wts[:, split:], labs[c, split:, :], preferred_element_type=jnp.float32
+            )
         mass[c] = part
         stage[c] = part.astype(jnp.bfloat16)
         if merge:
@@ -379,6 +411,7 @@
             pltpu.VMEM((nc, nb * rows, LANES), jnp.bfloat16),
             pltpu.VMEM((nb * nr, nq, LANES), jnp.float32),
             pltpu.VMEM((nq, LANES), jnp.float32),
+            pltpu.VMEM((2, nq, LANES), jnp.float32),
             pltpu.VMEM((nq, nb * rows), jnp.bfloat16),
             pltpu.VMEM((nc, nq, LANES), jnp.float32),
             pltpu.VMEM((nc, nq, LANES), jnp.bfloat16),

time: 38.6 us -> 37.8 us (0.979)
  Pallas kernels: 36.8 us -> 36 us
    pallas_call x1, Pallas kernels: 36.8 us -> 36 us  [per_device(): pl.pallas_call(functools.partial(kernel, ny, cores, nz, score_scale), out...]
where the time goes in v3:
time: 37.8 us; the launch traced here: 37.7 us
  Pallas kernels  36 us (95%)
  local copies, waits for them, and re-layouts  1.67 us (4%)
    pallas_call x1, Pallas kernels, per_device(): pl.pallas_call(functools.partial(kernel, ny, cores, nz, score_scale), out...  36 us
    unnamed x1, local copies, waits for them, and re-layouts  1.67 us

profile of v3, /device:TPU:0, one launch (start us, length us, event | category | flops | bytes accessed | tf_op | source)
XLA Modules:
  0.0 37.7 jit_solution(8430076974655384977)
XLA Ops:
  0.0 36.0 %shard_map.37 = f32[128,512]{1,0:T(8,128)} custom-call(bf16[512,1024]{1,0:T(8,128)(2,1)} %q_hbm.1, bf16[256,1024]{1,0:T(8,128)(2,1)} %r_hbm.1, bf16[256,512]{1,0:T(8,128)(2,1)} %l_hbm.1), custom_call_target="tpu_custom_call" | custom-call | tf_op jit(solution)/shard_map/pallas_call | solution.py:403
  36.0 1.7 %copy.5 = f32[128,512]{1,0:T(8,128)} copy(f32[128,512]{1,0:T(8,128)} %shard_map.37) | data formatting | bytes 524288
